TPU v7x, 128 devices: a whole 4x4x4 slice. The times are simulated.
128 devices in a mesh: row: 4 (over y_hi, core), col: 4 (over z), dp: 8 (over y_lo, x).
Axes of the slice: x: 4, y: 4 (y_hi: 2, y_lo: 2; y = y_hi * 2 + y_lo), z: 4, core: 2. Of those that a mesh axis runs over, the one named last changes fastest.
Arguments:
- observed: bfloat16 [4096, 2048], P(('row', 'dp'), 'col'), may hold values from -6 to 6
- next_observed: bfloat16 [4096, 2048], P(('row', 'dp'), 'col'), may hold values from -6 to 6
- actions: bfloat16 [4096, 128], P(('row', 'dp')), may hold values from -1 to 1
- next_mean: bfloat16 [4096, 128], P(('row', 'dp')), may hold values from -1.1953125 to 1.1953125
- policy_noise: float32 [4096, 128], P(('row', 'dp')), may hold values from -1.5 to 1.5
- rewards: bfloat16 [4096], P(('row', 'dp')), may hold values from -5 to 5
- discounts: bfloat16 [4096], P(('row', 'dp')), may hold values from 0.5 to 0.98828125
- actor_flags: int32 [4096], P(('row', 'dp')), may hold values 0 or 1
- critic_in: float32 [2, 2048, 2048], P(None, 'col', 'row'), may hold values from -0.125 to 0.125
- critic_act: float32 [2, 128, 2048], P(None, None, 'col'), may hold values from -0.5 to 0.5
- critic_head: float32 [2, 2048], P(None, 'row'), may hold values from -0.125 to 0.125
- target_in: float32 [2, 2048, 2048], P(None, 'col', 'row'), may hold values from -0.125 to 0.125
- target_act: float32 [2, 128, 2048], P(None, None, 'col'), may hold values from -0.5 to 0.5
- target_head: float32 [2, 2048], P(None, 'row'), may hold values from -0.125 to 0.125
Outputs:
- new_in: float32 [2, 2048, 2048], P(None, 'col', 'row')
- new_act: float32 [2, 128, 2048], P(None, None, 'col')
- new_head: float32 [2, 2048], P(None, 'row')
- new_target_in: float32 [2, 2048, 2048], P(None, 'col', 'row')
- new_target_act: float32 [2, 128, 2048], P(None, None, 'col')
- new_target_head: float32 [2, 2048], P(None, 'row')
- temporal_errors: float32 [2, 4096], P(None, ('row', 'dp'))
- action_slope: float32 [4096, 128], P(('row', 'dp'))
All inputs are finite; a program needn't handle non-finite values. No bound on the sum of `actor_flags` on one device may be relied on, other than what follows from the above.
Results may differ from a plain program's by a relative error of at most 0.008.
Values may be sent and summed in bfloat16 or wider, within the bound.
No kernel may reach another device: no remote copies, remote signals or barrier semaphores. Data moves between devices by JAX's collectives and lax.ppermute only.
A program may use at most 128 MiB of HBM per device.

v0:
```python
import math
import jax
import jax.numpy as jnp
from jax import lax
from jax.sharding import PartitionSpec as P

noise_clip = 0.5
matrix_rate = 0.004
head_rate = 0.0001
blend_rate = 0.005


def in_one_piece(arrays, axis, dim, along):
    widths = [math.prod(a.shape[along:]) for a in arrays]
    both = jnp.concatenate(
        [a.reshape(*a.shape[:along], w) for a, w in zip(arrays, widths)], axis=along
    )
    whole = lax.all_gather(both, axis, axis=dim, tiled=True)
    blocks = jnp.split(whole, [sum(widths[:k]) for k in range(1, len(widths))], axis=along)
    return tuple(
        (b.reshape(*whole.shape[:along], *a.shape[along:]) for a, b in zip(arrays, blocks))
    )


def in_one_piece_2(arrays, axis, dim, along):
    ends, at = ([], 0)
    for a in arrays[:-1]:
        at += a.shape[along]
        ends.append(at)
    both = jnp.concatenate(arrays, axis=along)
    return tuple(
        jnp.split(lax.psum_scatter(both, axis, scatter_dimension=dim, tiled=True), ends, axis=along)
    )


def sent_to_all(x, axis):
    copies = jnp.broadcast_to(x, (lax.axis_size(axis), *x.shape))
    return lax.all_to_all(copies, axis, split_axis=0, concat_axis=0, tiled=True)


def taken_together(x, axis):
    return sent_to_all(x, axis).sum(axis=0)


def packed_total(arrays, axis):
    ends = [0]
    for a in arrays:
        ends.append(ends[-1] + a.size)
    running = taken_together(jnp.concatenate([a.ravel() for a in arrays]), axis)
    return tuple((running[b:e].reshape(a.shape) for a, b, e in zip(arrays, ends, ends[1:])))


def in_one_piece_3(arrays, axis, dim, along):
    both = jnp.concatenate(arrays, axis=along)
    whole, at, gathered = (lax.all_gather(both, axis, axis=dim, tiled=True), 0, [])
    for a in arrays:
        gathered.append(lax.slice_in_dim(whole, at, at + a.shape[along], axis=along))
        at += a.shape[along]
    return tuple(gathered)


def rows_first(arrays, axis, dims):
    turned = [jnp.moveaxis(a, dim, 0) for a, dim in zip(arrays, dims)]
    widths = [t[0].size for t in turned]
    both = jnp.concatenate([t.reshape(-1, w) for t, w in zip(turned, widths)], axis=1)
    whole = lax.all_gather(both, axis, axis=0, tiled=True)
    blocks = jnp.split(whole, [sum(widths[:k]) for k in range(1, len(widths))], axis=1)
    return tuple(
        (
            jnp.moveaxis(b.reshape(-1, *t.shape[1:]), 0, dim)
            for b, t, dim in zip(blocks, turned, dims)
        )
    )


def silu_slope(preact):
    sigma = jax.nn.sigmoid(preact)
    return sigma * (1.0 + preact * (1.0 - sigma))


def embed(states, moves, weight_act):
    summed = states.astype(jnp.float32) + jnp.dot(
        moves, weight_act.astype(jnp.bfloat16), preferred_element_type=jnp.float32
    )
    return summed.astype(jnp.bfloat16)


def contract_rows(left, right):
    return lax.dot_general(
        left, right, (((0,), (0,)), ((), ())), preferred_element_type=jnp.float32
    )


def on_device(
    observed,
    next_observed,
    actions,
    next_mean,
    policy_noise,
    rewards,
    discounts,
    actor_flags,
    critic_in,
    critic_act,
    critic_head,
    target_in,
    target_act,
    target_head,
):
    noisy = jnp.clip(
        next_mean.astype(jnp.float32) + jnp.clip(policy_noise, -noise_clip, noise_clip), -1.0, 1.0
    ).astype(jnp.bfloat16)
    states, next_states, moves, next_moves, group_rewards, group_discounts = in_one_piece(
        (observed, next_observed, actions, noisy, rewards, discounts), "row", 0, 1
    )
    inner = [critic_in[which].astype(jnp.bfloat16) for which in range(2)]
    online = [embed(states, moves, critic_act[which]) for which in range(2)]
    shadow = [embed(next_states, next_moves, target_act[which]) for which in range(2)]
    partials = [
        jnp.dot(online[which], inner[which], preferred_element_type=jnp.float32)
        for which in range(2)
    ]
    partials += [
        jnp.dot(
            shadow[which], target_in[which].astype(jnp.bfloat16), preferred_element_type=jnp.float32
        )
        for which in range(2)
    ]
    total_rows = states.shape[0]
    preacts = tuple(
        (
            part.astype(jnp.float32)
            for part in in_one_piece_2(
                (
                    partials[0].astype(jnp.bfloat16),
                    partials[1].astype(jnp.bfloat16),
                    partials[2].astype(jnp.bfloat16),
                    partials[3].astype(jnp.bfloat16),
                ),
                "col",
                0,
                1,
            )
        )
    )
    row_count = total_rows // lax.axis_size("col")
    first_row = lax.axis_index("col") * row_count
    share_rewards = lax.dynamic_slice_in_dim(group_rewards, first_row, row_count).astype(
        jnp.float32
    )
    share_discounts = lax.dynamic_slice_in_dim(group_discounts, first_row, row_count).astype(
        jnp.float32
    )
    heads = [critic_head[0], critic_head[1], target_head[0], target_head[1]]
    hiddens = [jax.nn.silu(preacts[which]) for which in range(4)]
    value_terms = [
        jnp.dot(hiddens[which], heads[which], precision=lax.Precision.HIGHEST) for which in range(4)
    ]
    values = packed_total((value_terms[0], value_terms[1], value_terms[2], value_terms[3]), "row")
    goal = share_rewards + share_discounts * jnp.minimum(values[2], values[3])
    errors = [values[0] - goal, values[1] - goal]
    slopes = [
        (heads[which] * silu_slope(preacts[which])).astype(jnp.bfloat16) for which in range(2)
    ]
    head_grads = [
        jnp.dot(2.0 * errors[which], hiddens[which], precision=lax.Precision.HIGHEST)
        for which in range(2)
    ]
    slopes = list(in_one_piece_3((slopes[0], slopes[1]), "col", 0, 1))
    errors = list(rows_first((errors[0], errors[1]), "col", (0, 0)))
    head_grads = list(packed_total((head_grads[0], head_grads[1]), "col"))
    deltas = [
        (2.0 * errors[which][:, None] * slopes[which].astype(jnp.float32)).astype(jnp.bfloat16)
        for which in range(2)
    ]
    back_terms = [
        lax.dot_general(
            slopes[which],
            inner[which],
            (((1,), (1,)), ((), ())),
            preferred_element_type=jnp.float32,
        )
        for which in range(2)
    ]
    grad_ins = [contract_rows(online[which], deltas[which]) for which in range(2)]
    own_rows = observed.shape[0]
    own_first = lax.axis_index("row") * own_rows
    own_errors = [
        lax.dynamic_slice_in_dim(errors[which], own_first, own_rows) for which in range(2)
    ]
    backs = lax.psum((back_terms[0], back_terms[1]), "row")
    grad_embedded = [
        (2.0 * errors[which][:, None] * backs[which]).astype(jnp.bfloat16) for which in range(2)
    ]
    grad_acts = [contract_rows(moves, grad_embedded[which]) for which in range(2)]
    mine = lax.dynamic_slice_in_dim(backs[0], own_first, own_rows).astype(jnp.bfloat16)
    push_term = lax.dot_general(
        mine,
        critic_act[0].astype(jnp.bfloat16),
        (((1,), (1,)), ((), ())),
        preferred_element_type=jnp.float32,
    )
    action_slope = taken_together(push_term, "col") * actor_flags.astype(jnp.float32)[:, None]
    temporal_errors = jnp.stack(own_errors)
    olds = [
        critic_in[0],
        critic_in[1],
        critic_act[0],
        critic_act[1],
        critic_head[0],
        critic_head[1],
    ]
    rates = [matrix_rate, matrix_rate, matrix_rate, matrix_rate, head_rate, head_rate]
    summed = (
        lax.psum(grad_ins[0].astype(jnp.bfloat16), "dp").astype(jnp.float32),
        lax.psum(grad_ins[1].astype(jnp.bfloat16), "dp").astype(jnp.float32),
        lax.psum(grad_acts[0].astype(jnp.bfloat16), "dp").astype(jnp.float32),
        lax.psum(grad_acts[1].astype(jnp.bfloat16), "dp").astype(jnp.float32),
        lax.psum(head_grads[0].astype(jnp.bfloat16), "dp").astype(jnp.float32),
        lax.psum(head_grads[1].astype(jnp.bfloat16), "dp").astype(jnp.float32),
    )
    fresh = [olds[which] - rates[which] * summed[which] for which in range(6)]
    new_in = jnp.stack([fresh[0], fresh[1]])
    new_act = jnp.stack([fresh[2], fresh[3]])
    new_head = jnp.stack([fresh[4], fresh[5]])
    new_target_in = blend_rate * new_in + (1.0 - blend_rate) * target_in
    new_target_act = blend_rate * new_act + (1.0 - blend_rate) * target_act
    new_target_head = blend_rate * new_head + (1.0 - blend_rate) * target_head
    return (
        new_in,
        new_act,
        new_head,
        new_target_in,
        new_target_act,
        new_target_head,
        temporal_errors,
        action_slope,
    )


def solution(mesh):
    return jax.shard_map(
        on_device,
        mesh=mesh,
        in_specs=(
            P(("row", "dp"), "col"),
            P(("row", "dp"), "col"),
            P(("row", "dp"), None),
            P(("row", "dp"), None),
            P(("row", "dp"), None),
            P(("row", "dp")),
            P(("row", "dp")),
            P(("row", "dp")),
            P(None, "col", "row"),
            P(None, None, "col"),
            P(None, "row"),
            P(None, "col", "row"),
            P(None, None, "col"),
            P(None, "row"),
        ),
        out_specs=(
            P(None, "col", "row"),
            P(None, None, "col"),
            P(None, "row"),
            P(None, "col", "row"),
            P(None, None, "col"),
            P(None, "row"),
            P(None, ("row", "dp")),
            P(("row", "dp"), None),
        ),
        check_vma=False,
    )
```

profile of v0, /device:TPU:0, one launch (start us, length us, event | category | flops | bytes accessed | tf_op | source)
XLA Modules:
  0.0 270.5 jit_solution(15028285660459501925)
XLA Ops:
  7.2 0.8 copy.40
  8.0 0.8 copy.41
  8.8 0.9 clamp_convert_fusion
  9.6 1.8 concatenate.18
  11.5 1.1 convert.14
  12.7 2.8 %convert.15 = bf16[2,512,512]{2,1,0:T(8,128)(2,1)} convert(f32[2,512,512]{2,1,0:T(8,128)} %param.25) | non-fusion elementwise | flops 524288 | bytes 3145728 | tf_op jit(solution)/shard_map/convert.6
  15.5 21.6 %all-gather.3.cloned.1.call-done = bf16[512,1282]{1,0:T(8,128)(2,1)} async-done(((bf16[128,1282]{1,0:T(8,128)(2,1)}), bf16[512,1282]{1,0:T(8,128)(2,1)}) %all-gather.3.cloned.1.call-update) | async-done | bytes 1312784 | tf_op jit(solution)/shard_map/all_gather | solution.py:18
  37.1 1.4 fusion
  38.5 1.3 convolution_convert_fusion.5
  39.8 1.4 fusion.1
  41.2 0.8 copy-done.3
  42.0 1.3 convolution_convert_fusion.4
  43.3 2.7 %convolution_convert_fusion.2 = bf16[512,512]{0,1:T(8,128)(2,1)} fusion(bf16[2,512,512]{2,1,0:T(8,128)(2,1)} %convert.15, bf16[512,1282]{1,0:T(8,128)(2,1)} %all-gather.3.cloned.1.call-done, bf16[2,128,512]{2,1,0:T(8,128)(2,1)S(1)} %convert.14), kind=kOutput, calls=%fused_computation.13 | convolution fusion | flops 336592896 | bytes 1835008 | tf_op jit(solution)/shard_map/dot_general | solution.py:124
  46.0 2.7 %convolution_convert_fusion.3 = bf16[512,512]{0,1:T(8,128)(2,1)} fusion(bf16[2,512,512]{2,1,0:T(8,128)(2,1)} %convert.15, bf16[512,1282]{1,0:T(8,128)(2,1)} %all-gather.3.cloned.1.call-done, bf16[2,128,512]{2,1,0:T(8,128)(2,1)S(1)} %convert.14), kind=kOutput, calls=%fused_computation.14 | convolution fusion | flops 336592896 | bytes 1835008 | tf_op jit(solution)/shard_map/dot_general | solution.py:124
  48.7 3.0 %pad_maximum_fusion = bf16[512,2048]{0,1:T(8,128)(2,1)} fusion(bf16[512,512]{0,1:T(8,128)(2,1)} %convolution_convert_fusion.2, bf16[512,512]{0,1:T(8,128)(2,1)} %convolution_convert_fusion.3, bf16[512,512]{0,1:T(8,128)(2,1)} %convolution_convert_fusion.4, bf16[512,512]{0,1:T(8,128)(2,1)} %convolution_convert_fusion.5), kind=kLoop, calls=%fused_computation | loop fusion | flops 8388608 | bytes 4194304 | tf_op jit(solution)/shard_map/concatenate | solution.py:30
  51.7 3.9 %copy.48 = bf16[512,2048]{1,0:T(8,128)(2,1)} copy(bf16[512,2048]{0,1:T(8,128)(2,1)} %pad_maximum_fusion) | data formatting | bytes 4194304
  56.3 28.8 %reduce-scatter.4.cloned.1.call-done = bf16[128,2048]{1,0:T(8,128)(2,1)} async-done(((bf16[512,2048]{1,0:T(8,128)(2,1)}), bf16[128,2048]{1,0:T(8,128)(2,1)}) %reduce-scatter.4.cloned.1.call-update) | async-done | bytes 524304 | tf_op jit(solution)/shard_map/reduce_scatter | solution.py:32
  85.1 1.2 fusion.30
  86.3 0.7 pad_maximum_fusion.3
  87.1 1.3 convolution_bitcast_fusion.3
  88.4 1.3 convolution_bitcast_fusion.1
  91.1 4.3 %all-to-all-start = ((f32[4,1,512]{2,1,0:T(1,128)}), f32[4,1,512]{2,1,0:T(1,128)S(1)}, u32[]{:S(2)}, u32[]{:S(2)}) async-start(f32[4,1,512]{2,1,0:T(1,128)} %broadcast_in_dim.10), calls=%async_computation | async-start | bytes 16384 | tf_op jit(solution)/shard_map/all_to_all | solution.py:38
  95.4 1.1 fusion.82
  96.6 4.1 %all-to-all-done = f32[4,1,512]{2,1,0:T(1,128)S(1)} async-done(((f32[4,1,512]{2,1,0:T(1,128)}), f32[4,1,512]{2,1,0:T(1,128)S(1)}, u32[]{:S(2)}, u32[]{:S(2)}) %all-to-all-start) | async-done | bytes 8224 | tf_op jit(solution)/shard_map/all_to_all | solution.py:38
  100.7 10.5 %all-gather.5.cloned.1.call-done = bf16[512,1024]{1,0:T(8,128)(2,1)} async-done(((bf16[128,1024]{1,0:T(8,128)(2,1)}), bf16[512,1024]{1,0:T(8,128)(2,1)}) %all-gather.5.cloned.1.call-update) | async-done | bytes 1048592 | tf_op jit(solution)/shard_map/all_gather | solution.py:55
  111.2 2.6 fusion.13
  113.8 1.4 fusion.10
  115.3 1.2 fusion.49
  116.5 1.2 fusion.50
  117.7 0.6 broadcast_in_dim.11
  118.3 3.5 %all-to-all-start.1 = ((f32[4,1,1024]{2,1,0:T(1,128)}), f32[4,1,1024]{2,1,0:T(1,128)S(1)}, u32[]{:S(2)}, u32[]{:S(2)}) async-start(f32[4,1,1024]{2,1,0:T(1,128)} %broadcast_in_dim.11), calls=%async_computation.1 | async-start | bytes 32768 | tf_op jit(solution)/shard_map/all_to_all | solution.py:38
  121.9 10.2 %all_gather.10 = f32[512,2]{0,1:T(2,128)S(1)} all-gather(f32[128,2]{0,1:T(2,128)S(1)} %pad_maximum_fusion.7), channel_id=1, replica_groups=mesh['row'=4,'col'=4,'dp'=8] {'col'}, dimensions={0}, use_global_device_ids=true | all-gather | bytes 5120 | tf_op jit(solution)/shard_map/all_gather | solution.py:66
  132.7 2.6 convolution_convert_fusion
  135.3 1.3 convolution_convert_fusion.1
  136.6 38.3 %all-reduce.6.cloned.1.call-done = (f32[512,512]{1,0:T(8,128)}, f32[512,512]{1,0:T(8,128)}) async-done(((f32[512,512]{1,0:T(8,128)}, f32[512,512]{1,0:T(8,128)}), (f32[512,512]{1,0:T(8,128)}, f32[512,512]{1,0:T(8,128)})) %all-reduce.6.cloned.1.call-update) | async-done | bytes 2097168 | tf_op jit(solution)/shard_map/psum | solution.py:191
  175.0 2.3 convolution_convert_fusion.6
  177.3 2.3 convolution_convert_fusion.7
  179.6 18.8 %all-reduce.1 = (bf16[512]{0:T(512)(128)(2,1)S(1)}, bf16[512]{0:T(512)(128)(2,1)S(1)}) all-reduce(bf16[512]{0:T(512)(128)(2,1)S(1)} %get-tuple-element.39, bf16[512]{0:T(512)(128)(2,1)S(1)} %get-tuple-element.38), channel_id=1, replica_groups=mesh['row'=4,'col'=4,'dp'=8] {'dp'}, use_global_device_ids=true, to_apply=%region_10.11 | all-reduce | flops 1024 | bytes 4096 | tf_op jit(solution)/shard_map/psum | solution.py:220
  198.4 1.1 fusion.40
  199.6 0.7 broadcast_in_dim.12
  200.3 4.4 %all-to-all-start.2 = ((f32[4,128,128]{2,1,0:T(8,128)}), f32[4,128,128]{2,1,0:T(8,128)S(1)}, u32[]{:S(2)}, u32[]{:S(2)}) async-start(f32[4,128,128]{2,1,0:T(8,128)} %broadcast_in_dim.12), calls=%async_computation.2 | async-start | bytes 524288 | tf_op jit(solution)/shard_map/all_to_all | solution.py:38
  205.3 6.1 %all-to-all-done.2 = f32[4,128,128]{2,1,0:T(8,128)S(1)} async-done(((f32[4,128,128]{2,1,0:T(8,128)}), f32[4,128,128]{2,1,0:T(8,128)S(1)}, u32[]{:S(2)}, u32[]{:S(2)}) %all-to-all-start.2) | async-done | bytes 262176 | tf_op jit(solution)/shard_map/all_to_all | solution.py:38
  211.4 0.7 broadcast_multiply_fusion
  212.1 45.5 %all-reduce.8.cloned.1.call-done = (bf16[512,512]{1,0:T(8,128)(2,1)}, bf16[512,512]{1,0:T(8,128)(2,1)}, bf16[128,512]{1,0:T(8,128)(2,1)}, bf16[128,512]{1,0:T(8,128)(2,1)}) async-done(((bf16[512,512]{1,0:T(8,128)(2,1)}, bf16[512,512]{1,0:T(8,128)(2,1)}, bf16[128,512]{1,0:T(8,128)(2,1)}, bf16[128,512]{1,0:T(8,128)(2,1)}), (bf16[512,512]{1,0:T(8,128)(2,1)}, bf16[512,512]{1,0:T(8,128)(2,1)}, ...) | async-done | bytes 1310736 | tf_op jit(solution)/shard_map/psum | solution.py:216
  257.6 1.1 fusion.39
  258.7 1.1 multiply_add_fusion.1
  260.2 1.2 copy-done.1
  261.4 2.5 multiply_add_fusion
  (58 shorter events, 4.1 us)
Async XLA Ops:
  7.2 29.9 %all-gather.3.cloned.1.call-start = ((), (), s32[]{:S(2)}) async-start(), calls=%async_computation.4 | async-start | bytes 1802240 | tf_op jit(solution)/shard_map/all_gather | solution.py:18
  11.4 25.6 %copy-start.2 = (f32[2,128,512]{2,1,0:T(8,128)S(1)}, f32[2,128,512]{2,1,0:T(8,128)}, u32[]{:S(2)}) copy-start(f32[2,128,512]{2,1,0:T(8,128)} %param.23) | copy-start | bytes 1572868
  11.5 73.6 %reduce-scatter.4.cloned.1.call-start = ((), (), s32[]{:S(2)}) async-start(), calls=%async_computation.6 | async-start | bytes 2621440 | tf_op jit(solution)/shard_map/reduce_scatter | solution.py:32
  12.6 25.8 %copy-start = (f32[2,512,512]{2,1,0:T(8,128)S(1)}, f32[2,512,512]{2,1,0:T(8,128)}, u32[]{:S(2)}) copy-start(f32[2,512,512]{2,1,0:T(8,128)} %param.22) | copy-start | bytes 6291460
  41.2 0.8 copy-start.3
  55.6 0.7 copy-start.10
  55.6 31.4 %copy-start.12 = (s32[128]{0:T(128)S(1)}, s32[128]{0:T(128)}, u32[]{:S(2)}) copy-start(s32[128]{0:T(128)} %param.21) | copy-start | bytes 1540
  55.6 32.8 %copy-start.11 = (f32[2,512]{1,0:T(2,128)S(1)}, f32[2,512]{1,0:T(2,128)}, u32[]{:S(2)}) copy-start(f32[2,512]{1,0:T(2,128)} %param.27) | copy-start | bytes 12292
  55.6 55.6 %all-gather.5.cloned.1.call-start = ((), (), s32[]{:S(2)}) async-start(), calls=%async_computation.5 | async-start | bytes 1310720 | tf_op jit(solution)/shard_map/all_gather | solution.py:55
  87.0 2.6 copy-start.9
  91.1 9.6 %all-to-all-start = ((f32[4,1,512]{2,1,0:T(1,128)}), f32[4,1,512]{2,1,0:T(1,128)S(1)}, u32[]{:S(2)}, u32[]{:S(2)}) async-start(f32[4,1,512]{2,1,0:T(1,128)} %broadcast_in_dim.10), calls=%async_computation | async-start | bytes 16384 | tf_op jit(solution)/shard_map/all_to_all | solution.py:38
  95.4 79.6 %all-reduce.6.cloned.1.call-start = ((), (), s32[]{:S(2)}) async-start(), calls=%async_computation.7 | async-start | bytes 4194304 | tf_op jit(solution)/shard_map/psum | solution.py:191
  111.2 2.6 copy-start.5
  118.3 14.3 %all-to-all-start.1 = ((f32[4,1,1024]{2,1,0:T(1,128)}), f32[4,1,1024]{2,1,0:T(1,128)S(1)}, u32[]{:S(2)}, u32[]{:S(2)}) async-start(f32[4,1,1024]{2,1,0:T(1,128)} %broadcast_in_dim.11), calls=%async_computation.1 | async-start | bytes 32768 | tf_op jit(solution)/shard_map/all_to_all | solution.py:38
  121.8 135.7 %all-reduce.8.cloned.1.call-start = ((), (), s32[]{:S(2)}) async-start(), calls=%async_computation.8 | async-start | bytes 2621440 | tf_op jit(solution)/shard_map/psum | solution.py:216
  132.7 2.6 copy-start.6
  179.5 79.2 %copy-start.4 = (f32[2,128,512]{2,1,0:T(8,128)S(1)}, f32[2,128,512]{2,1,0:T(8,128)}, u32[]{:S(2)}) copy-start(f32[2,128,512]{2,1,0:T(8,128)} %param.26) | copy-start | bytes 1572868
  200.3 11.1 %all-to-all-start.2 = ((f32[4,128,128]{2,1,0:T(8,128)}), f32[4,128,128]{2,1,0:T(8,128)S(1)}, u32[]{:S(2)}, u32[]{:S(2)}) async-start(f32[4,128,128]{2,1,0:T(8,128)} %broadcast_in_dim.12), calls=%async_computation.2 | async-start | bytes 524288 | tf_op jit(solution)/shard_map/all_to_all | solution.py:38
  257.6 2.3 copy-start.7
  257.6 2.3 copy-start.8
  259.8 1.6 copy-start.1
Sparse Core Ops, SparseCore 0:
  11.6 25.4 all-gather.2
  55.8 29.2 reduce-scatter.3
  87.4 23.7 all-gather.4
  115.4 59.5 all-reduce.5
  179.7 77.8 all-reduce.7
where the time goes:
time: 271 us; the launch traced here: 270 us
  waiting for transfers between devices  155 us (57%)
  matrix products  30.3 us (11%)
  blocking collectives  29 us (11%)
  other arithmetic  17 us (6%)
  between operations  14 us (5%)
  local copies, waits for them, and re-layouts  13 us (5%)
  starting transfers between devices  12.3 us (5%)
    psum x1, waiting for transfers between devices, on_device(): lax.psum(grad_ins[1].astype(jnp.bfloat16), 'dp').astype(jnp.float32)  45.5 us
    psum x1, waiting for transfers between devices, on_device(): backs = lax.psum((back_terms[0], back_terms[1]), 'row')  38.3 us
    reduce_scatter x1, waiting for transfers between devices, in_one_piece_2(): lax.psum_scatter(both, axis, scatter_dimension=dim, tiled=True)  28.8 us
    all_gather x1, waiting for transfers between devices, in_one_piece(): whole = lax.all_gather(both, axis, axis=dim, tiled=True)  21.6 us
    psum x1, blocking collectives, on_device(): lax.psum(head_grads[1].astype(jnp.bfloat16), 'dp').astype(jnp.float32)  18.8 us
    all_to_all x3, starting transfers between devices, sent_to_all(): return lax.all_to_all(copies, axis, split_axis=0, concat_axis=0, tiled=True)  12.2 us
    all_gather x1, waiting for transfers between devices, in_one_piece_3(): lax.all_gather(both, axis, axis=dim, tiled=True)  10.5 us
    all_gather x1, blocking collectives, rows_first(): whole = lax.all_gather(both, axis, axis=0, tiled=True)  10.2 us
  transfers between devices with their start and end apart: 8, of which 7 were waited for; matrix products, arithmetic and copies ran while one was open for 7% of the time, Pallas kernels for 0%

commit v1 on v0

--- a/solution.py
+++ b/solution.py
@@ -63,7 +63,8 @@
     turned = [jnp.moveaxis(a, dim, 0) for a, dim in zip(arrays, dims)]
     widths = [t[0].size for t in turned]
     both = jnp.concatenate([t.reshape(-1, w) for t, w in zip(turned, widths)], axis=1)
-    whole = lax.all_gather(both, axis, axis=0, tiled=True)
+    sent = jnp.stack([both] * lax.axis_size(axis))
+    whole = jnp.concatenate(lax.all_to_all(sent, axis, 0, 0), axis=0)
     blocks = jnp.split(whole, [sum(widths[:k]) for k in range(1, len(widths))], axis=1)
     return tuple(
         (

time: 271 us -> 272 us (level)
  blocking collectives: 29 us -> 18.8 us
  waiting for transfers between devices: 155 us -> 161 us
  starting transfers between devices: 12.3 us -> 15.6 us
    all_gather x1 -> x0, blocking collectives: 10.2 us -> none  [rows_first(): whole = lax.all_gather(both, axis, axis=0, tiled=True)]
    all_to_all x3, waiting for transfers between devices: 10.2 us -> 14.8 us  [sent_to_all(): return lax.all_to_all(copies, axis, split_axis=0, concat_axis=0, tiled=True)]
    all_to_all x0 -> x1, starting transfers between devices: none -> 3.49 us  [rows_first(): whole = jnp.concatenate(lax.all_to_all(sent, axis, 0, 0), axis=0)]
    all_to_all x0 -> x1, waiting for transfers between devices: none -> 2.88 us  [rows_first(): whole = jnp.concatenate(lax.all_to_all(sent, axis, 0, 0), axis=0)]
  transfers between devices with their start and end apart: 8 -> 9, of which waited for: 7 -> 9; matrix products, arithmetic and copies ran while one was open for 7% -> 8% of each run, Pallas kernels for 0% -> 0%
where the time goes in v1:
time: 272 us; the launch traced here: 271 us
  waiting for transfers between devices  161 us (59%)
  matrix products  30.3 us (11%)
  blocking collectives  18.8 us (7%)
  other arithmetic  17 us (6%)
  starting transfers between devices  15.6 us (6%)
  between operations  14 us (5%)
  local copies, waits for them, and re-layouts  13.6 us (5%)
    psum x1, waiting for transfers between devices, on_device(): lax.psum(grad_ins[1].astype(jnp.bfloat16), 'dp').astype(jnp.float32)  45.5 us
    psum x1, waiting for transfers between devices, on_device(): backs = lax.psum((back_terms[0], back_terms[1]), 'row')  37.1 us
    reduce_scatter x1, waiting for transfers between devices, in_one_piece_2(): lax.psum_scatter(both, axis, scatter_dimension=dim, tiled=True)  28.8 us
    all_gather x1, waiting for transfers between devices, in_one_piece(): whole = lax.all_gather(both, axis, axis=dim, tiled=True)  21.6 us
    psum x1, blocking collectives, on_device(): lax.psum(head_grads[1].astype(jnp.bfloat16), 'dp').astype(jnp.float32)  18.8 us
    all_to_all x3, waiting for transfers between devices, sent_to_all(): return lax.all_to_all(copies, axis, split_axis=0, concat_axis=0, tiled=True)  14.8 us
    all_to_all x3, starting transfers between devices, sent_to_all(): return lax.all_to_all(copies, axis, split_axis=0, concat_axis=0, tiled=True)  12 us
    all_gather x1, waiting for transfers between devices, in_one_piece_3(): lax.all_gather(both, axis, axis=dim, tiled=True)  10.5 us
  transfers between devices with their start and end apart: 9, of which 9 were waited for; matrix products, arithmetic and copies ran while one was open for 8% of the time, Pallas kernels for 0%

profile of v1, /device:TPU:0, one launch (start us, length us, event | category | flops | bytes accessed | tf_op | source)
XLA Modules:
  0.0 270.5 jit_solution(12267112437382745263)
XLA Ops:
  7.2 0.8 copy.40
  8.0 0.8 copy.41
  8.8 0.9 clamp_convert_fusion
  9.6 1.8 concatenate.18
  11.5 1.1 convert.14
  12.7 2.8 %convert.15 = bf16[2,512,512]{2,1,0:T(8,128)(2,1)} convert(f32[2,512,512]{2,1,0:T(8,128)} %param.25) | non-fusion elementwise | flops 524288 | bytes 3145728 | tf_op jit(solution)/shard_map/convert.6
  15.5 21.6 %all-gather.3.cloned.1.call-done = bf16[512,1282]{1,0:T(8,128)(2,1)} async-done(((bf16[128,1282]{1,0:T(8,128)(2,1)}), bf16[512,1282]{1,0:T(8,128)(2,1)}) %all-gather.3.cloned.1.call-update) | async-done | bytes 1312784 | tf_op jit(solution)/shard_map/all_gather | solution.py:18
  37.1 1.4 fusion
  38.5 1.3 convolution_convert_fusion.5
  39.8 1.4 fusion.1
  41.2 0.8 copy-done.3
  42.0 1.3 convolution_convert_fusion.4
  43.3 2.7 %convolution_convert_fusion.2 = bf16[512,512]{0,1:T(8,128)(2,1)} fusion(bf16[2,512,512]{2,1,0:T(8,128)(2,1)} %convert.15, bf16[512,1282]{1,0:T(8,128)(2,1)} %all-gather.3.cloned.1.call-done, bf16[2,128,512]{2,1,0:T(8,128)(2,1)S(1)} %convert.14), kind=kOutput, calls=%fused_computation.13 | convolution fusion | flops 336592896 | bytes 1835008 | tf_op jit(solution)/shard_map/dot_general | solution.py:125
  46.0 2.7 %convolution_convert_fusion.3 = bf16[512,512]{0,1:T(8,128)(2,1)} fusion(bf16[2,512,512]{2,1,0:T(8,128)(2,1)} %convert.15, bf16[512,1282]{1,0:T(8,128)(2,1)} %all-gather.3.cloned.1.call-done, bf16[2,128,512]{2,1,0:T(8,128)(2,1)S(1)} %convert.14), kind=kOutput, calls=%fused_computation.14 | convolution fusion | flops 336592896 | bytes 1835008 | tf_op jit(solution)/shard_map/dot_general | solution.py:125
  48.7 3.0 %pad_maximum_fusion = bf16[512,2048]{0,1:T(8,128)(2,1)} fusion(bf16[512,512]{0,1:T(8,128)(2,1)} %convolution_convert_fusion.2, bf16[512,512]{0,1:T(8,128)(2,1)} %convolution_convert_fusion.3, bf16[512,512]{0,1:T(8,128)(2,1)} %convolution_convert_fusion.4, bf16[512,512]{0,1:T(8,128)(2,1)} %convolution_convert_fusion.5), kind=kLoop, calls=%fused_computation | loop fusion | flops 8388608 | bytes 4194304 | tf_op jit(solution)/shard_map/concatenate | solution.py:30
  51.7 3.9 %copy.48 = bf16[512,2048]{1,0:T(8,128)(2,1)} copy(bf16[512,2048]{0,1:T(8,128)(2,1)} %pad_maximum_fusion) | data formatting | bytes 4194304
  56.3 28.8 %reduce-scatter.4.cloned.1.call-done = bf16[128,2048]{1,0:T(8,128)(2,1)} async-done(((bf16[512,2048]{1,0:T(8,128)(2,1)}), bf16[128,2048]{1,0:T(8,128)(2,1)}) %reduce-scatter.4.cloned.1.call-update) | async-done | bytes 524304 | tf_op jit(solution)/shard_map/reduce_scatter | solution.py:32
  85.1 1.2 fusion.30
  86.2 0.7 pad_maximum_fusion.3
  87.0 1.3 convolution_bitcast_fusion.3
  88.4 1.3 convolution_bitcast_fusion.1
  91.1 4.3 %all-to-all-start = ((f32[4,1,512]{2,1,0:T(1,128)}), f32[4,1,512]{2,1,0:T(1,128)S(1)}, u32[]{:S(2)}, u32[]{:S(2)}) async-start(f32[4,1,512]{2,1,0:T(1,128)} %broadcast_in_dim.10), calls=%async_computation | async-start | bytes 16384 | tf_op jit(solution)/shard_map/all_to_all | solution.py:38
  95.4 1.1 fusion.82
  96.6 4.1 %all-to-all-done = f32[4,1,512]{2,1,0:T(1,128)S(1)} async-done(((f32[4,1,512]{2,1,0:T(1,128)}), f32[4,1,512]{2,1,0:T(1,128)S(1)}, u32[]{:S(2)}, u32[]{:S(2)}) %all-to-all-start) | async-done | bytes 8224 | tf_op jit(solution)/shard_map/all_to_all | solution.py:38
  100.7 10.5 %all-gather.5.cloned.1.call-done = bf16[512,1024]{1,0:T(8,128)(2,1)} async-done(((bf16[128,1024]{1,0:T(8,128)(2,1)}), bf16[512,1024]{1,0:T(8,128)(2,1)}) %all-gather.5.cloned.1.call-update) | async-done | bytes 1048592 | tf_op jit(solution)/shard_map/all_gather | solution.py:55
  111.2 2.6 fusion.13
  113.8 1.4 fusion.10
  115.9 3.5 %all-to-all-start.1 = ((f32[4,128,2]{1,2,0:T(2,128)}), f32[4,128,2]{1,2,0:T(2,128)S(1)}, u32[]{:S(2)}, u32[]{:S(2)}) async-start(f32[4,128,2]{1,2,0:T(2,128)} %stack.43), calls=%async_computation.1 | async-start | bytes 8192 | tf_op jit(solution)/shard_map/all_to_all | solution.py:67
  119.4 1.2 fusion.49
  120.6 1.2 fusion.50
  121.8 2.9 %all-to-all-done.1 = f32[4,128,2]{1,2,0:T(2,128)S(1)} async-done(((f32[4,128,2]{1,2,0:T(2,128)}), f32[4,128,2]{1,2,0:T(2,128)S(1)}, u32[]{:S(2)}, u32[]{:S(2)}) %all-to-all-start.1) | async-done | bytes 4128 | tf_op jit(solution)/shard_map/all_to_all | solution.py:67
  125.3 3.3 %all-to-all-start.2 = ((f32[4,1,1024]{2,1,0:T(1,128)}), f32[4,1,1024]{2,1,0:T(1,128)S(1)}, u32[]{:S(2)}, u32[]{:S(2)}) async-start(f32[4,1,1024]{2,1,0:T(1,128)} %broadcast_in_dim.11), calls=%async_computation.2 | async-start | bytes 32768 | tf_op jit(solution)/shard_map/all_to_all | solution.py:38
  129.2 4.7 %all-to-all-done.2 = f32[4,1,1024]{2,1,0:T(1,128)S(1)} async-done(((f32[4,1,1024]{2,1,0:T(1,128)}), f32[4,1,1024]{2,1,0:T(1,128)S(1)}, u32[]{:S(2)}, u32[]{:S(2)}) %all-to-all-start.2) | async-done | bytes 16416 | tf_op jit(solution)/shard_map/all_to_all | solution.py:38
  133.9 2.6 convolution_convert_fusion
  136.6 1.3 convolution_convert_fusion.1
  137.9 37.1 %all-reduce.6.cloned.1.call-done = (f32[512,512]{1,0:T(8,128)}, f32[512,512]{1,0:T(8,128)}) async-done(((f32[512,512]{1,0:T(8,128)}, f32[512,512]{1,0:T(8,128)}), (f32[512,512]{1,0:T(8,128)}, f32[512,512]{1,0:T(8,128)})) %all-reduce.6.cloned.1.call-update) | async-done | bytes 2097168 | tf_op jit(solution)/shard_map/psum | solution.py:192
  175.0 2.3 convolution_convert_fusion.6
  177.3 2.3 convolution_convert_fusion.7
  179.6 18.8 %all-reduce.1 = (bf16[512]{0:T(512)(128)(2,1)S(1)}, bf16[512]{0:T(512)(128)(2,1)S(1)}) all-reduce(bf16[512]{0:T(512)(128)(2,1)S(1)} %get-tuple-element.39, bf16[512]{0:T(512)(128)(2,1)S(1)} %get-tuple-element.38), channel_id=1, replica_groups=mesh['row'=4,'col'=4,'dp'=8] {'dp'}, use_global_device_ids=true, to_apply=%region_10.11 | all-reduce | flops 1024 | bytes 4096 | tf_op jit(solution)/shard_map/psum | solution.py:221
  198.5 1.1 fusion.40
  199.6 0.7 broadcast_in_dim.12
  200.3 4.4 %all-to-all-start.3 = ((f32[4,128,128]{2,1,0:T(8,128)}), f32[4,128,128]{2,1,0:T(8,128)S(1)}, u32[]{:S(2)}, u32[]{:S(2)}) async-start(f32[4,128,128]{2,1,0:T(8,128)} %broadcast_in_dim.12), calls=%async_computation.3 | async-start | bytes 524288 | tf_op jit(solution)/shard_map/all_to_all | solution.py:38
  205.3 6.1 %all-to-all-done.3 = f32[4,128,128]{2,1,0:T(8,128)S(1)} async-done(((f32[4,128,128]{2,1,0:T(8,128)}), f32[4,128,128]{2,1,0:T(8,128)S(1)}, u32[]{:S(2)}, u32[]{:S(2)}) %all-to-all-start.3) | async-done | bytes 262176 | tf_op jit(solution)/shard_map/all_to_all | solution.py:38
  212.2 45.5 %all-reduce.8.cloned.1.call-done = (bf16[512,512]{1,0:T(8,128)(2,1)}, bf16[512,512]{1,0:T(8,128)(2,1)}, bf16[128,512]{1,0:T(8,128)(2,1)}, bf16[128,512]{1,0:T(8,128)(2,1)}) async-done(((bf16[512,512]{1,0:T(8,128)(2,1)}, bf16[512,512]{1,0:T(8,128)(2,1)}, bf16[128,512]{1,0:T(8,128)(2,1)}, bf16[128,512]{1,0:T(8,128)(2,1)}), (bf16[512,512]{1,0:T(8,128)(2,1)}, bf16[512,512]{1,0:T(8,128)(2,1)}, ...) | async-done | bytes 1310736 | tf_op jit(solution)/shard_map/psum | solution.py:217
  257.6 1.1 fusion.39
  258.8 1.1 multiply_add_fusion.1
  260.3 1.2 copy-done.1
  261.5 2.5 multiply_add_fusion
  (60 shorter events, 6.1 us)
Async XLA Ops:
  7.2 29.9 %all-gather.3.cloned.1.call-start = ((), (), s32[]{:S(2)}) async-start(), calls=%async_computation.5 | async-start | bytes 1802240 | tf_op jit(solution)/shard_map/all_gather | solution.py:18
  11.4 25.6 %copy-start.2 = (f32[2,128,512]{2,1,0:T(8,128)S(1)}, f32[2,128,512]{2,1,0:T(8,128)}, u32[]{:S(2)}) copy-start(f32[2,128,512]{2,1,0:T(8,128)} %param.23) | copy-start | bytes 1572868
  11.5 73.6 %reduce-scatter.4.cloned.1.call-start = ((), (), s32[]{:S(2)}) async-start(), calls=%async_computation.7 | async-start | bytes 2621440 | tf_op jit(solution)/shard_map/reduce_scatter | solution.py:32
  12.6 25.8 %copy-start = (f32[2,512,512]{2,1,0:T(8,128)S(1)}, f32[2,512,512]{2,1,0:T(8,128)}, u32[]{:S(2)}) copy-start(f32[2,512,512]{2,1,0:T(8,128)} %param.22) | copy-start | bytes 6291460
  41.2 0.8 copy-start.3
  55.6 0.7 copy-start.10
  55.6 31.4 %copy-start.12 = (s32[128]{0:T(128)S(1)}, s32[128]{0:T(128)}, u32[]{:S(2)}) copy-start(s32[128]{0:T(128)} %param.21) | copy-start | bytes 1540
  55.6 32.8 %copy-start.11 = (f32[2,512]{1,0:T(2,128)S(1)}, f32[2,512]{1,0:T(2,128)}, u32[]{:S(2)}) copy-start(f32[2,512]{1,0:T(2,128)} %param.27) | copy-start | bytes 12292
  55.6 55.6 %all-gather.5.cloned.1.call-start = ((), (), s32[]{:S(2)}) async-start(), calls=%async_computation.6 | async-start | bytes 1310720 | tf_op jit(solution)/shard_map/all_gather | solution.py:55
  87.0 2.6 copy-start.9
  91.1 9.6 %all-to-all-start = ((f32[4,1,512]{2,1,0:T(1,128)}), f32[4,1,512]{2,1,0:T(1,128)S(1)}, u32[]{:S(2)}, u32[]{:S(2)}) async-start(f32[4,1,512]{2,1,0:T(1,128)} %broadcast_in_dim.10), calls=%async_computation | async-start | bytes 16384 | tf_op jit(solution)/shard_map/all_to_all | solution.py:38
  95.4 79.6 %all-reduce.6.cloned.1.call-start = ((), (), s32[]{:S(2)}) async-start(), calls=%async_computation.8 | async-start | bytes 4194304 | tf_op jit(solution)/shard_map/psum | solution.py:192
  111.2 2.6 copy-start.5
  115.9 8.8 %all-to-all-start.1 = ((f32[4,128,2]{1,2,0:T(2,128)}), f32[4,128,2]{1,2,0:T(2,128)S(1)}, u32[]{:S(2)}, u32[]{:S(2)}) async-start(f32[4,128,2]{1,2,0:T(2,128)} %stack.43), calls=%async_computation.1 | async-start | bytes 8192 | tf_op jit(solution)/shard_map/all_to_all | solution.py:67
  125.3 8.6 %all-to-all-start.2 = ((f32[4,1,1024]{2,1,0:T(1,128)}), f32[4,1,1024]{2,1,0:T(1,128)S(1)}, u32[]{:S(2)}, u32[]{:S(2)}) async-start(f32[4,1,1024]{2,1,0:T(1,128)} %broadcast_in_dim.11), calls=%async_computation.2 | async-start | bytes 32768 | tf_op jit(solution)/shard_map/all_to_all | solution.py:38
  128.6 129.1 %all-reduce.8.cloned.1.call-start = ((), (), s32[]{:S(2)}) async-start(), calls=%async_computation.9 | async-start | bytes 2621440 | tf_op jit(solution)/shard_map/psum | solution.py:217
  133.9 2.6 copy-start.6
  179.6 79.2 %copy-start.4 = (f32[2,128,512]{2,1,0:T(8,128)S(1)}, f32[2,128,512]{2,1,0:T(8,128)}, u32[]{:S(2)}) copy-start(f32[2,128,512]{2,1,0:T(8,128)} %param.26) | copy-start | bytes 1572868
  200.3 11.1 %all-to-all-start.3 = ((f32[4,128,128]{2,1,0:T(8,128)}), f32[4,128,128]{2,1,0:T(8,128)S(1)}, u32[]{:S(2)}, u32[]{:S(2)}) async-start(f32[4,128,128]{2,1,0:T(8,128)} %broadcast_in_dim.12), calls=%async_computation.3 | async-start | bytes 524288 | tf_op jit(solution)/shard_map/all_to_all | solution.py:38
  257.6 2.3 copy-start.7
  257.6 2.3 copy-start.8
  259.9 1.6 copy-start.1
Sparse Core Ops, SparseCore 0:
  11.6 25.4 all-gather.2
  55.7 29.2 reduce-scatter.3
  87.4 23.7 all-gather.4
  115.4 59.5 all-reduce.5
  179.7 77.8 all-reduce.7
